TPU v7x, 32 devices: a whole 2x2x4 slice. The times are simulated.
32 devices in a mesh: parts: 2 (over x), docs: 16 (over z, y, core).
Axes of the slice: x: 2, y: 2, z: 4, core: 2. Of those that a mesh axis runs over, the one named last changes fastest.
Arguments:
- doc_grads: bfloat16 [4096, 8192], P('parts', 'docs'), parts along dimension 0, may hold values from -6 to 6
- query_grads: bfloat16 [16384, 8192], P(('parts', 'docs')), parts along dimension 0, may hold values from -6 to 6
- left_inv: bfloat16 [2, 32, 32], replicated, may hold values from -17 to 17, as said below
- right_inv: bfloat16 [2, 128, 128], replicated, may hold values from -17 to 17, as said below
- cand_owner: int32 [8192, 1], P(('parts', 'docs')), parts along dimension 0, may hold values from 0 to 15; in each aligned block of 256 rows (0 to 255, 256 to 511, ...) at most 32 rows name the same one
- cand_row: int32 [8192], P(('parts', 'docs')), parts along dimension 0, may hold values from 0 to 127
Outputs:
- scores: float32 [16384, 256], P(('parts', 'docs')), parts along dimension 0
There are 2 independent parts, one for each index of `parts`. A program takes and returns all parts, laid end to end along the dimension named above; an argument that names none is the same for every part. Nothing has to cross between parts.
Inputs may be any that keep to these rules, and one draw needn't show every extreme that they name: `cand_owner`: within the 256 entries of one query batch no owner is named more than 32 times, a bound that some block reaches. `left_inv`: symmetric positive definite. `right_inv`: symmetric positive definite.
All inputs are finite; a program needn't handle non-finite values.
Results may differ from a plain program's by a relative error of at most 0.004.
Values may be sent and summed in bfloat16 or wider, within the bound.
No kernel may reach another device: no remote copies, remote signals or barrier semaphores. Data moves between devices by JAX's collectives and lax.ppermute only.
A program may use at most 128 MiB of HBM per device.

v0:
```python
import jax
import jax.numpy as jnp
from jax import lax
from jax.experimental import pallas as pl
from jax.experimental.pallas import tpu as pltpu
from jax.sharding import PartitionSpec as P

LANES = 128
SUBLANES = 8
MXU = 256
VMEM_BYTES = 48 << 20


def call(kernel, out_shape, grid, in_specs, out_specs, flops, bytes_accessed, scratch=(), prefetch=0):
    return pl.pallas_call(
        kernel,
        grid_spec=pltpu.PrefetchScalarGridSpec(
            num_scalar_prefetch=prefetch,
            grid=grid,
            in_specs=in_specs,
            out_specs=out_specs,
            scratch_shapes=scratch,
        ),
        out_shape=out_shape,
        compiler_params=pltpu.CompilerParams(vmem_limit_bytes=VMEM_BYTES),
        cost_estimate=pl.CostEstimate(flops=flops, bytes_accessed=bytes_accessed, transcendentals=0),
    )


def dot(a, b):
    return jnp.dot(a, b, preferred_element_type=jnp.float32)


def one_hot(ids, docs):
    group, row = ids // LANES, ids % LANES
    in_group = (lax.broadcasted_iota(jnp.int32, (LANES, ids.shape[1]), 0) == row).astype(jnp.bfloat16)
    return jnp.concatenate(
        [in_group * (group == g).astype(jnp.bfloat16) for g in range(docs // LANES)], axis=0
    )


def gather_rows(base, ids, tables, count):
    entries = ids.shape[2]
    docs = tables[0].shape[1]
    features = sum(t.shape[0] for t in tables)

    def kernel(base_ref, ids_ref, *refs):
        out_ref = refs[-1]
        hot = one_hot(ids_ref[0], docs)
        start = 0
        for table_ref in refs[:-1]:
            stop = start + table_ref.shape[0]
            out_ref[0, start:stop, :] = dot(table_ref[...], hot).astype(out_ref.dtype)
            start = stop

    return call(
        kernel,
        pltpu.HBM((count, features, entries), tables[0].dtype),
        (count,),
        [pl.BlockSpec((1, 1, entries), lambda b, base: (base[0] + b, 0, 0))]
        + [pl.BlockSpec(t.shape, lambda b, base: (0, 0)) for t in tables],
        pl.BlockSpec((1, features, entries), lambda b, base: (b, 0, 0)),
        1000,
        1000,
        prefetch=1,
    )(base, ids, *tables)


def gather_pieces(me, ids, tables, partners):
    entries = ids.shape[2]
    docs = tables[0][0].shape[1]
    features = sum(rows for _, rows in tables)
    count = len(partners)

    def kernel(me_ref, *refs):
        table_refs = refs[count : count + len(tables)]
        for ids_ref, out_ref in zip(refs[:count], refs[count + len(tables) :]):
            hot = one_hot(ids_ref[0], docs)
            start = 0
            for table_ref in table_refs:
                stop = start + table_ref.shape[0]
                out_ref[start:stop, :] = dot(table_ref[...], hot).astype(out_ref.dtype)
                start = stop

    return call(
        kernel,
        [pltpu.HBM((features, entries), tables[0][0].dtype)] * count,
        (1,),
        [pl.BlockSpec((1, 1, entries), lambda i, me, k=k: (me[0] ^ k, 0, 0)) for k in partners]
        + [pl.BlockSpec((rows, docs), lambda i, me: (0, 0)) for _, rows in tables],
        [pl.BlockSpec((features, entries), lambda i, me: (0, 0))] * count,
        2 * count * features * docs * entries,
        2 * features * (docs + count * entries),
        prefetch=1,
    )(me, *[ids] * count, *[table for table, _ in tables])


def padded(values, above, below):
    zeros = lambda rows: [jnp.zeros((rows, values.shape[1]), values.dtype)] if rows else []
    return jnp.concatenate([*zeros(above), values, *zeros(below)], axis=0)


def score_pieces(me, prepared, far, near, total, width, half, scale):
    queries = prepared.shape[0]
    entries = next(iter({**far, **near}.values())).shape[1]
    prepared_specs, chosen, depth = [], [], 0
    for k, piece in far.items():
        prepared_specs.append(pl.BlockSpec((queries, width), lambda i, me, k=k: (0, me[0] ^ k)))
        chosen.append(piece)
        depth += piece.shape[0]
    for k, piece in near.items():
        tail = piece.shape[0] - width
        block = max(tail, LANES)
        stride = width // block
        prepared_specs.append(pl.BlockSpec((queries, width), lambda i, me, k=k: (0, me[0] ^ k)))
        prepared_specs.append(
            pl.BlockSpec(
                (queries, block), lambda i, me, k=k: (0, (me[0] ^ k ^ half) * stride + stride - 1)
            )
        )
        chosen.append(piece)
        depth += piece.shape[0]
    totals = [] if total is None else [total]
    whole = pl.BlockSpec((queries, entries), lambda i, me: (0, 0))

    def kernel(me_ref, *refs):
        prepared_refs = iter(refs[: len(prepared_specs)])
        chosen_refs = iter(refs[len(prepared_specs) : len(prepared_specs) + len(chosen)])
        parts = [ref[...] for ref in refs[len(prepared_specs) + len(chosen) : -1]]
        for _ in far:
            piece = next(chosen_refs)[...]
            parts.append(dot(next(prepared_refs)[...], padded(piece, 0, width - piece.shape[0])))
        for _ in near:
            piece = next(chosen_refs)[...]
            parts.append(dot(next(prepared_refs)[...], piece[:width]))
            rest = next(prepared_refs)[...]
            parts.append(dot(rest, padded(piece[width:], rest.shape[1] - piece.shape[0] + width, 0)))
        refs[-1][...] = sum(parts[1:], parts[0]) * scale

    return call(
        kernel,
        jax.ShapeDtypeStruct((queries, entries), jnp.float32),
        (1,),
        prepared_specs
        + [pl.BlockSpec(piece.shape, lambda i, me: (0, 0)) for piece in chosen]
        + [whole] * len(totals),
        whole,
        2 * queries * depth * entries,
        2 * depth * (queries + entries) + 8 * queries * entries,
        prefetch=1,
    )(me, *[prepared] * len(prepared_specs), *chosen, *totals)


def score_all(prepared, chosen, scale):
    queries = prepared.shape[0]
    devices, width, entries = chosen.shape

    def kernel(prepared_ref, chosen_ref, out_ref):
        part = dot(prepared_ref[...], chosen_ref[...]) * scale

        @pl.when(pl.program_id(0) == 0)
        def _():
            out_ref[...] = part

        @pl.when(pl.program_id(0) > 0)
        def _():
            out_ref[...] += part

    steps = 4
    block = devices * width // steps
    return call(
        kernel,
        jax.ShapeDtypeStruct((queries, entries), jnp.float32),
        (steps,),
        [
            pl.BlockSpec((queries, block), lambda i: (0, i)),
            pl.BlockSpec((block, entries), lambda i: (i, 0)),
        ],
        pl.BlockSpec((queries, entries), lambda i: (0, 0)),
        2 * devices * width * queries * entries,
        2 * devices * width * (queries + entries) + 4 * queries * entries,
    )(prepared, chosen.reshape(devices * width, entries))


def precondition(queries, left_inv, right_inv):
    total, features = queries.shape
    layers, k_out, _ = left_inv.shape
    k_in = right_inv.shape[1]
    group = MXU // k_out
    pair = MXU // k_in
    rows = 64
    wide = k_out // pair
    both = 2 * group

    def spread(values, times):
        size = values.shape[0]
        rows = lax.broadcasted_iota(jnp.int32, (MXU, size), 0) // times
        picks = (rows == lax.broadcasted_iota(jnp.int32, (MXU, size), 1)).astype(values.dtype)
        wide = dot(picks, values).astype(values.dtype)
        wide = lax.dot_general(
            wide, picks, (((1,), (1,)), ((), ())), preferred_element_type=jnp.float32
        )
        row = lax.broadcasted_iota(jnp.int32, (MXU, MXU), 0) % times
        column = lax.broadcasted_iota(jnp.int32, (MXU, MXU), 1) % times
        return jnp.where(row == column, wide, 0.0).astype(values.dtype)

    def repeat(values, times):
        empty = jnp.zeros_like(values)
        return jnp.concatenate(
            [
                jnp.concatenate([values if i == j else empty for j in range(times)], axis=1)
                for i in range(times)
            ],
            axis=0,
        )

    def kernel(queries_ref, left_inv_ref, right_inv_ref, out_ref, middle_ref, left_ref, right_ref):
        @pl.when(pl.program_id(0) == 0)
        def _():
            for layer in range(layers):
                left_ref[layer] = spread(left_inv_ref[layer], group)
                right_ref[layer] = repeat(right_inv_ref[layer], pair)

        for layer in range(layers):
            first = layer * k_out * k_in
            stack = jnp.concatenate(
                [queries_ref[:, first + p * MXU : first + (p + 1) * MXU] for p in range(wide)], axis=0
            )
            middle_ref[...] = dot(stack, right_ref[layer])
            for q in range(0, rows, both):
                halves = []
                for start in (q, q + group):
                    tiles = []
                    for p in range(wide):
                        at = p * rows + start
                        for s in range(pair):
                            tiles.append(middle_ref[at : at + group, s * k_in : (s + 1) * k_in])
                    halves.append(jnp.concatenate(tiles, axis=0))
                middle = jnp.concatenate(halves, axis=1).astype(queries_ref.dtype)
                result = dot(left_ref[layer], middle)
                for a in range(k_out):
                    at = a * group
                    tile = jnp.concatenate(
                        [result[at : at + group, :k_in], result[at : at + group, k_in:]], axis=0
                    )
                    lanes = first + a * k_in
                    out_ref[q : q + both, lanes : lanes + k_in] = tile.astype(out_ref.dtype)

    return call(
        kernel,
        jax.ShapeDtypeStruct(queries.shape, queries.dtype),
        (total // rows,),
        [
            pl.BlockSpec((rows, features), lambda i: (i, 0)),
            pl.BlockSpec(left_inv.shape, lambda i: (0, 0, 0)),
            pl.BlockSpec(right_inv.shape, lambda i: (0, 0, 0)),
        ],
        pl.BlockSpec((rows, features), lambda i: (i, 0)),
        4 * total * features * MXU,
        4 * total * features,
        scratch=[
            pltpu.VMEM((wide * rows, MXU), jnp.float32),
            pltpu.VMEM((layers, MXU, MXU), left_inv.dtype),
            pltpu.VMEM((layers, MXU, MXU), right_inv.dtype),
        ],
    )(queries, left_inv, right_inv)


def after(value, *earlier):
    return lax.optimization_barrier((value, *earlier))[0]


def on_device(doc_grads, query_grads, left_inv, right_inv, cand_owner, cand_row):
    devices = lax.axis_size("docs")
    half = devices // 2
    me = lax.axis_index("docs").astype(jnp.int32).reshape(1)
    base = me & -half
    doc_count = doc_grads.shape[0] // devices
    entries = cand_row.shape[0]
    width = doc_grads.shape[1]
    scale = query_grads.shape[1] ** (-0.5)

    def swap(values, k):
        return lax.ppermute(values, "docs", [(i, i ^ k) for i in range(devices)])

    tail = width // 8 if width % (4 * LANES) == 0 else 0
    table = doc_grads.T
    if tail:
        across = swap(table[width - tail :], half)
    own_ids = cand_owner[:, 0] * doc_count + cand_row
    ids = lax.all_to_all(
        jnp.broadcast_to(own_ids, (devices, 1, entries)), "docs", split_axis=0, concat_axis=0, tiled=True
    )
    if not tail:
        picked = gather_rows(jnp.zeros((1,), jnp.int32), ids, [table], devices)
        chosen = lax.all_to_all(picked, "docs", split_axis=0, concat_axis=0, tiled=True)
        return score_all(precondition(query_grads, left_inv, right_inv), chosen, scale)

    first, flight = 2, 5
    far = list(range(half, devices))
    near = [*range(half // 2, half), *range(half // 2 - 1, 0, -1)]
    inside = [0, *near]
    body = [(table, width - tail)]
    order = far[:first]
    rest = [far[first:-1], list(near)]
    while any(rest):
        order += [part.pop(0) for part in rest if part]
    order.append(far[-1])
    ids = after(ids, across)
    pieces = dict(zip(far, gather_pieces(me, ids, body, far[:first])))
    ids = after(ids, pieces[order[0]])
    pieces.update(zip(inside, gather_pieces(me, ids, [(table, width), (across, tail)], inside)))
    ids = after(ids, pieces[0])
    pieces.update(zip(far[first:], gather_pieces(me, ids, body, far[first:])))
    came = {0: pieces[0]}
    for position, k in enumerate(order):
        piece = pieces[k]
        if position >= first:
            before = [came[j] for j in order[:first]]
            if position >= flight + first:
                before = [came[order[position - flight]]]
            piece = after(piece, *before)
        came[k] = swap(piece, k)
    prepared = precondition(after(query_grads, came[order[first - 1]]), left_inv, right_inv)

    total = None
    stops = [0, len(order) - 5, len(order) - 1, len(order)]
    for start, stop in zip(stops, stops[1:]):
        keys = [*([0] if start == 0 else []), *order[start:stop]]
        total = score_pieces(
            me,
            prepared,
            {k: came[k] for k in keys if k >= half},
            {k: came[k] for k in keys if k < half},
            total,
            width,
            half,
            scale if stop == len(order) else 1.0,
        )
    return total


def solution(mesh):
    placed = (
        P("parts", "docs"),
        P(("parts", "docs"), None),
        P(),
        P(),
        P(("parts", "docs"), None),
        P(("parts", "docs")),
    )
    return jax.shard_map(
        on_device, mesh=mesh, in_specs=placed, out_specs=P(("parts", "docs"), None), check_vma=False
    )
```

profile of v0, /device:TPU:25, one launch (start us, length us, event | category | flops | bytes accessed | tf_op | source)
XLA Modules:
  0.0 129.9 jit_solution(7443183025871732487)
XLA Ops:
  0.0 2.9 %copy.7 = bf16[2048,512]{0,1:T(8,128)(2,1)S(1)} copy(bf16[2048,512]{1,0:T(8,128)(2,1)} %param.6) | data formatting | bytes 4194304 | tf_op args[0]
  3.0 0.1 collective-permute-start
  3.1 0.7 broadcast_multiply_fusion
  3.8 0.7 add.3
  4.4 0.6 broadcast_in_dim.3
  5.1 6.9 %all-to-all-start = ((s32[16,1,256]{2,1,0:T(1,128)}), s32[16,1,256]{2,1,0:T(1,128)S(1)}, u32[]{:S(2)}, u32[]{:S(2)}) async-start(s32[16,1,256]{2,1,0:T(1,128)} %broadcast_in_dim.3), calls=%async_computation | async-start | bytes 32768 | tf_op jit(solution)/shard_map/all_to_all | solution.py:291
  12.0 7.0 %all-to-all-done.refs_0_.refs_1_.refs_2_.refs_3_.refs_4_.refs_5_.refs_6_.refs_7_ = s32[16,1,256]{2,1,0:T(1,128)S(1)} async-done(((s32[16,1,256]{2,1,0:T(1,128)}), s32[16,1,256]{2,1,0:T(1,128)S(1)}, u32[]{:S(2)}, u32[]{:S(2)}) %all-to-all-start) | async-done | bytes 16416 | tf_op jit(solution)/shard_map/all_to_all | solution.py:291
  19.0 0.0 collective-permute-done.refs_9_
  19.0 1.9 %shard_map.64 = (bf16[448,256]{1,0:T(8,128)(2,1)}, bf16[448,256]{1,0:T(8,128)(2,1)}) custom-call(s32[1]{0:T(128)} %bitcast.me_ref, s32[16,1,256]{2,1,0:T(1,128)S(1)} %all-to-all-done.refs_0_.refs_1_.refs_2_.refs_3_.refs_4_.refs_5_.refs_6_.refs_7_, s32[16,1,256]{2,1,0:T(1,128)S(1)} %all-to-all-done.refs_0_.refs_1_.refs_2_.refs_3_.refs_4_.refs_5_.refs_6_.refs_7_, ...), custom_call_target="tpu_custom_call" | custom-call | flops 939524096 | bytes 2293760 | tf_op jit(solution)/shard_map/pallas_call | solution.py:85
  20.9 0.0 collective-permute-start.2
  20.9 2.9 %collective-permute-start.1 = (bf16[448,256]{1,0:T(8,128)(2,1)}, bf16[448,256]{1,0:T(8,128)(2,1)S(1)}, u32[]{:S(2)}, u32[]{:S(2)}) collective-permute-start(bf16[448,256]{1,0:T(8,128)(2,1)} %get-tuple-element.39), channel_id=1, source_target_pairs={{0,9},{1,8},{2,11},{3,10},{4,13},{5,12},{6,15},{7,14},{8,1},{9,0},... | collective-permute-start | bytes 688136 | tf_op jit(solution)/shard_map/ppermute | solution.py:284
  23.8 6.9 %shard_map.66 = (bf16[576,256]{1,0:T(8,128)(2,1)}, bf16[576,256]{1,0:T(8,128)(2,1)}, bf16[576,256]{1,0:T(8,128)(2,1)}, bf16[576,256]{1,0:T(8,128)(2,1)}, bf16[57...) custom-call(s32[1]{0:T(128)} %bitcast.me_ref, ...), custom_call_target="tpu_custom_call" | custom-call | flops 4831838208 | bytes 4718592 | tf_op jit(solution)/shard_map/pallas_call | solution.py:85
  30.7 0.0 copy-start.9
  30.7 0.0 copy-start.8
  30.7 0.0 copy-start.7
  30.7 0.0 copy-start.6
  30.7 0.0 copy-start.5
  30.7 0.0 copy-start.4
  30.8 0.0 copy-start.3
  30.8 0.0 copy-start.1
  30.8 0.0 copy-start.2
  30.8 3.9 %shard_map.67 = (bf16[448,256]{1,0:T(8,128)(2,1)}, bf16[448,256]{1,0:T(8,128)(2,1)}, bf16[448,256]{1,0:T(8,128)(2,1)}, bf16[448,256]{1,0:T(8,128)(2,1)}, bf16[44...) custom-call(s32[1]{0:T(128)} %bitcast.me_ref, ...), custom_call_target="tpu_custom_call" | custom-call | flops 2818572288 | bytes 3211264 | tf_op jit(solution)/shard_map/pallas_call | solution.py:85
  34.7 9.5 %collective-permute-done.1.refs_17_ = bf16[448,256]{1,0:T(8,128)(2,1)S(1)} collective-permute-done((bf16[448,256]{1,0:T(8,128)(2,1)}, bf16[448,256]{1,0:T(8,128)(2,1)S(1)}, u32[]{:S(2)}, u32[]{:S(2)}) %collective-permute-start.1) | collective-permute-done | bytes 229408 | tf_op jit(solution)/shard_map/ppermute | solution.py:284
  44.2 0.0 collective-permute-done.2.refs_16_
  44.2 0.0 collective-permute-start.3
  44.2 3.6 %collective-permute-start.10 = (bf16[448,256]{1,0:T(8,128)(2,1)}, bf16[448,256]{1,0:T(8,128)(2,1)S(1)}, u32[]{:S(2)}, u32[]{:S(2)}) collective-permute-start(bf16[448,256]{1,0:T(8,128)(2,1)} %get-tuple-element.62), channel_id=1, source_target_pairs={{0,10},{1,11},{2,8},{3,9},{4,14},{5,15},{6,12},{7,13},{8,2},{9,3},... | collective-permute-start | bytes 688136 | tf_op jit(solution)/shard_map/ppermute | solution.py:284
  47.8 0.0 copy-done.9
  47.8 0.0 collective-permute-start.13
  47.8 0.0 copy-done.8
  47.8 2.0 %collective-permute-start.6 = (bf16[576,256]{1,0:T(8,128)(2,1)S(1)}, bf16[576,256]{1,0:T(8,128)(2,1)S(1)}, u32[]{:S(2)}, u32[]{:S(2)}) collective-permute-start(bf16[576,256]{1,0:T(8,128)(2,1)S(1)} %copy-done.8), channel_id=1, source_target_pairs={{0,5},{1,4},{2,7},{3,6},{4,1},{5,0},{6,3},{7,2},{8,13},{9,12},{10,... | collective-permute-start | bytes 884744 | tf_op jit(solution)/shard_map/ppermute | solution.py:284
  49.8 10.9 %collective-permute-done.3.refs_19_ = bf16[448,256]{1,0:T(8,128)(2,1)S(1)} collective-permute-done((bf16[448,256]{1,0:T(8,128)(2,1)}, bf16[448,256]{1,0:T(8,128)(2,1)S(1)}, u32[]{:S(2)}, u32[]{:S(2)}) %collective-permute-start.3) | collective-permute-done | bytes 229408 | tf_op jit(solution)/shard_map/ppermute | solution.py:284
  60.7 0.0 copy-done.7
  60.7 1.1 collective-permute-start.4
  61.8 3.8 %collective-permute-done.10.refs_18_ = bf16[448,256]{1,0:T(8,128)(2,1)S(1)} collective-permute-done((bf16[448,256]{1,0:T(8,128)(2,1)}, bf16[448,256]{1,0:T(8,128)(2,1)S(1)}, u32[]{:S(2)}, u32[]{:S(2)}) %collective-permute-start.10) | collective-permute-done | bytes 229408 | tf_op jit(solution)/shard_map/ppermute | solution.py:284
  65.6 0.0 copy-done.6
  65.6 0.0 collective-permute-start.11
  65.6 1.9 %collective-permute-start.8 = (bf16[448,256]{1,0:T(8,128)(2,1)}, bf16[448,256]{1,0:T(8,128)(2,1)S(1)}, u32[]{:S(2)}, u32[]{:S(2)}) collective-permute-start(bf16[448,256]{1,0:T(8,128)(2,1)} %get-tuple-element.57), channel_id=1, source_target_pairs={{0,12},{1,13},{2,14},{3,15},{4,8},{5,9},{6,10},{7,11},{8,4},{9,5},... | collective-permute-start | bytes 688136 | tf_op jit(solution)/shard_map/ppermute | solution.py:284
  67.6 0.0 collective-permute-done.13.refs_23_
  67.6 2.2 %collective-permute-start.14 = (bf16[448,256]{1,0:T(8,128)(2,1)}, bf16[448,256]{1,0:T(8,128)(2,1)S(1)}, u32[]{:S(2)}, u32[]{:S(2)}) collective-permute-start(bf16[448,256]{1,0:T(8,128)(2,1)} %get-tuple-element.69), channel_id=1, source_target_pairs={{0,13},{1,12},{2,15},{3,14},{4,9},{5,8},{6,11},{7,10},{8,5},{9,4},... | collective-permute-start | bytes 688136 | tf_op jit(solution)/shard_map/ppermute | solution.py:284
  69.8 15.9 %collective-permute-done.8.refs_20_ = bf16[448,256]{1,0:T(8,128)(2,1)S(1)} collective-permute-done((bf16[448,256]{1,0:T(8,128)(2,1)}, bf16[448,256]{1,0:T(8,128)(2,1)S(1)}, u32[]{:S(2)}, u32[]{:S(2)}) %collective-permute-start.8) | collective-permute-done | bytes 229408 | tf_op jit(solution)/shard_map/ppermute | solution.py:284
  85.7 0.0 copy-done.5
  85.7 1.0 collective-permute-start.9
  86.7 0.0 collective-permute-done.6.refs_24_
  86.7 4.4 %collective-permute-start.7 = (bf16[448,256]{1,0:T(8,128)(2,1)}, bf16[448,256]{1,0:T(8,128)(2,1)S(1)}, u32[]{:S(2)}, u32[]{:S(2)}) collective-permute-start(bf16[448,256]{1,0:T(8,128)(2,1)} %get-tuple-element.54), channel_id=1, source_target_pairs={{0,14},{1,15},{2,12},{3,13},{4,10},{5,11},{6,8},{7,9},{8,6},{9,7},... | collective-permute-start | bytes 688136 | tf_op jit(solution)/shard_map/ppermute | solution.py:284
  91.1 0.0 collective-permute-done.4.refs_26_
  91.1 0.2 collective-permute-start.5
  91.3 13.2 %collective-permute-done.11.refs_25_ = bf16[576,256]{1,0:T(8,128)(2,1)S(1)} collective-permute-done((bf16[576,256]{1,0:T(8,128)(2,1)S(1)}, bf16[576,256]{1,0:T(8,128)(2,1)S(1)}, u32[]{:S(2)}, u32[]{:S(2)}) %collective-permute-start.11) | collective-permute-done | bytes 294944 | tf_op jit(solution)/shard_map/ppermute | solution.py:284
  104.5 0.0 copy-done.4
  104.5 1.1 collective-permute-start.12
  105.6 0.0 collective-permute-done.14.refs_21_
  105.6 0.0 copy-done.3
  105.6 1.6 %collective-permute-start.15 = (bf16[576,256]{1,0:T(8,128)(2,1)S(1)}, bf16[576,256]{1,0:T(8,128)(2,1)S(1)}, u32[]{:S(2)}, u32[]{:S(2)}) collective-permute-start(bf16[576,256]{1,0:T(8,128)(2,1)S(1)} %copy-done.3), channel_id=1, source_target_pairs={{0,1},{1,0},{2,3},{3,2},{4,5},{5,4},{6,7},{7,6},{8,9},{9,8},{10,11... | collective-permute-start | bytes 884744 | tf_op jit(solution)/shard_map/ppermute | solution.py:284
  107.2 0.0 copy-done.1
  107.2 0.0 copy-done.2
  107.2 13.1 %shard_map.65.refs_0_.refs_1_.refs_2_.refs_3_.refs_4_.refs_5_.refs_6_.refs_7_.refs_8_.refs_9_.refs_10_.refs_11_.refs_12_.refs_13_.refs_14_.refs_15_ = bf16[512,8192]{1,0:T(8,128)(2,1)} custom-call(bf16[512,8192]{1,0:T(8,128)(2,1)} %queries_ref, bf16[2,32,32]{2,1,0:T(8,128)(2,1)S(1)} %copy-done.2, bf16[2,128,128]{2,1,0:T(8,128)(2,1)S(1)} %copy-done.1), custom_call_target="tpu_custom_call" | custom-call | flops 4294967296 | bytes 16777216 | tf_op jit(solution)/shard_map/pallas_call | solution.py:249
  120.3 0.0 copy-done
  120.3 4.8 %shard_map.68.refs_11_ = f32[512,256]{1,0:T(8,128)S(1)} custom-call(s32[1]{0:T(128)} %bitcast.me_ref, bf16[512,8192]{1,0:T(8,128)(2,1)} %shard_map.65.refs_0_.refs_1_.refs_2_.refs_3_.refs_4_.refs_5_.refs_6_.refs_7_.refs_8_.refs_9_.refs_10_.refs_11_.refs_12_.refs_13_.refs_14_.refs_15_, ...), custom_call_target="tpu_custom_call" | custom-call | flops 1459617792 | bytes 9601024 | tf_op jit(solution)/shard_map/pallas_call | solution.py:140
  125.1 0.0 collective-permute-done.9.refs_8_
  125.1 0.0 collective-permute-done.7.refs_7_
  125.2 0.0 collective-permute-done.12.refs_9_
  125.2 0.0 collective-permute-done.15.refs_10_
  125.2 2.5 %shard_map.69.refs_2_ = f32[512,256]{1,0:T(8,128)S(1)} custom-call(s32[1]{0:T(128)} %bitcast.me_ref, bf16[512,8192]{1,0:T(8,128)(2,1)} %shard_map.65.refs_0_.refs_1_.refs_2_.refs_3_.refs_4_.refs_5_.refs_6_.refs_7_.refs_8_.refs_9_.refs_10_.refs_11_.refs_12_.refs_13_.refs_14_.refs_15_, ...), custom_call_target="tpu_custom_call" | custom-call | flops 570425344 | bytes 4390912 | tf_op jit(solution)/shard_map/pallas_call | solution.py:140
  127.7 0.0 collective-permute-done.5.refs_1_
  127.7 2.1 %shard_map.70 = f32[512,256]{1,0:T(8,128)} custom-call(s32[1]{0:T(128)} %bitcast.me_ref, bf16[512,8192]{1,0:T(8,128)(2,1)} %shard_map.65.refs_0_.refs_1_.refs_2_.refs_3_.refs_4_.refs_5_.refs_6_.refs_7_.refs_8_.refs_9_.refs_10_.refs_11_.refs_12_.refs_13_.refs_14_.refs_15_, bf16[448,256]{1,0:T(8,128)(2,1)S(1)} %collective-permute-done.5.refs_1_, ...), custom_call_target="tpu_custom_call" | custom-call | flops 117440512 | bytes 1736704 | tf_op jit(solution)/shard_map/pallas_call | solution.py:140
  (2 shorter events, 0.0 us)
Async XLA Ops:
  3.0 16.0 %collective-permute-start = (bf16[64,2048]{1,0:T(8,128)(2,1)S(1)}, bf16[64,2048]{1,0:T(8,128)(2,1)S(1)}, u32[]{:S(2)}, u32[]{:S(2)}) collective-permute-start(bf16[64,2048]{1,0:T(8,128)(2,1)S(1)} %slice.4), channel_id=1, source_target_pairs={{0,8},{1,9},{2,10},{3,11},{4,12},{5,13},{6,14},{7,15},{8,0},{9,1},... | collective-permute-start | bytes 786440 | tf_op jit(solution)/shard_map/ppermute | solution.py:284
  5.1 13.9 %all-to-all-start = ((s32[16,1,256]{2,1,0:T(1,128)}), s32[16,1,256]{2,1,0:T(1,128)S(1)}, u32[]{:S(2)}, u32[]{:S(2)}) async-start(s32[16,1,256]{2,1,0:T(1,128)} %broadcast_in_dim.3), calls=%async_computation | async-start | bytes 32768 | tf_op jit(solution)/shard_map/all_to_all | solution.py:291
  20.9 23.3 %collective-permute-start.2 = (bf16[448,256]{1,0:T(8,128)(2,1)}, bf16[448,256]{1,0:T(8,128)(2,1)S(1)}, u32[]{:S(2)}, u32[]{:S(2)}) collective-permute-start(bf16[448,256]{1,0:T(8,128)(2,1)} %get-tuple-element.41), channel_id=1, source_target_pairs={{0,8},{1,9},{2,10},{3,11},{4,12},{5,13},{6,14},{7,15},{8,0},{9,1},... | collective-permute-start | bytes 688136 | tf_op jit(solution)/shard_map/ppermute | solution.py:284
  20.9 23.3 %collective-permute-start.1 = (bf16[448,256]{1,0:T(8,128)(2,1)}, bf16[448,256]{1,0:T(8,128)(2,1)S(1)}, u32[]{:S(2)}, u32[]{:S(2)}) collective-permute-start(bf16[448,256]{1,0:T(8,128)(2,1)} %get-tuple-element.39), channel_id=1, source_target_pairs={{0,9},{1,8},{2,11},{3,10},{4,13},{5,12},{6,15},{7,14},{8,1},{9,0},... | collective-permute-start | bytes 688136 | tf_op jit(solution)/shard_map/ppermute | solution.py:284
  30.7 17.1 %copy-start.9 = (bf16[576,256]{1,0:T(8,128)(2,1)S(1)}, bf16[576,256]{1,0:T(8,128)(2,1)}, u32[]{:S(2)}) copy-start(bf16[576,256]{1,0:T(8,128)(2,1)} %get-tuple-element.68) | copy-start | bytes 884740
  30.7 17.1 %copy-start.8 = (bf16[576,256]{1,0:T(8,128)(2,1)S(1)}, bf16[576,256]{1,0:T(8,128)(2,1)}, u32[]{:S(2)}) copy-start(bf16[576,256]{1,0:T(8,128)(2,1)} %get-tuple-element.53) | copy-start | bytes 884740
  30.7 30.0 %copy-start.7 = (bf16[576,256]{1,0:T(8,128)(2,1)S(1)}, bf16[576,256]{1,0:T(8,128)(2,1)}, u32[]{:S(2)}) copy-start(bf16[576,256]{1,0:T(8,128)(2,1)} %get-tuple-element.49) | copy-start | bytes 884740
  30.7 34.9 %copy-start.6 = (bf16[576,256]{1,0:T(8,128)(2,1)S(1)}, bf16[576,256]{1,0:T(8,128)(2,1)}, u32[]{:S(2)}) copy-start(bf16[576,256]{1,0:T(8,128)(2,1)} %get-tuple-element.63) | copy-start | bytes 884740
  30.7 55.0 %copy-start.5 = (bf16[576,256]{1,0:T(8,128)(2,1)S(1)}, bf16[576,256]{1,0:T(8,128)(2,1)}, u32[]{:S(2)}) copy-start(bf16[576,256]{1,0:T(8,128)(2,1)} %get-tuple-element.58) | copy-start | bytes 884740
  30.7 73.8 %copy-start.4 = (bf16[576,256]{1,0:T(8,128)(2,1)S(1)}, bf16[576,256]{1,0:T(8,128)(2,1)}, u32[]{:S(2)}) copy-start(bf16[576,256]{1,0:T(8,128)(2,1)} %get-tuple-element.64) | copy-start | bytes 884740
  30.8 74.8 %copy-start.3 = (bf16[576,256]{1,0:T(8,128)(2,1)S(1)}, bf16[576,256]{1,0:T(8,128)(2,1)}, u32[]{:S(2)}) copy-start(bf16[576,256]{1,0:T(8,128)(2,1)} %get-tuple-element.70) | copy-start | bytes 884740
  30.8 76.4 %copy-start.1 = (bf16[2,128,128]{2,1,0:T(8,128)(2,1)S(1)}, bf16[2,128,128]{2,1,0:T(8,128)(2,1)}, u32[]{:S(2)}) copy-start(bf16[2,128,128]{2,1,0:T(8,128)(2,1)} %right_inv_ref.1) | copy-start | bytes 196612
  30.8 76.4 %copy-start.2 = (bf16[2,32,32]{2,1,0:T(8,128)(2,1)S(1)}, bf16[2,32,32]{2,1,0:T(8,128)(2,1)}, u32[]{:S(2)}) copy-start(bf16[2,32,32]{2,1,0:T(8,128)(2,1)} %left_inv_ref.1) | copy-start | bytes 12292
  44.2 16.5 %collective-permute-start.3 = (bf16[448,256]{1,0:T(8,128)(2,1)}, bf16[448,256]{1,0:T(8,128)(2,1)S(1)}, u32[]{:S(2)}, u32[]{:S(2)}) collective-permute-start(bf16[448,256]{1,0:T(8,128)(2,1)} %get-tuple-element.48), channel_id=1, source_target_pairs={{0,11},{1,10},{2,9},{3,8},{4,15},{5,14},{6,13},{7,12},{8,3},{9,2},... | collective-permute-start | bytes 688136 | tf_op jit(solution)/shard_map/ppermute | solution.py:284
  44.2 21.4 %collective-permute-start.10 = (bf16[448,256]{1,0:T(8,128)(2,1)}, bf16[448,256]{1,0:T(8,128)(2,1)S(1)}, u32[]{:S(2)}, u32[]{:S(2)}) collective-permute-start(bf16[448,256]{1,0:T(8,128)(2,1)} %get-tuple-element.62), channel_id=1, source_target_pairs={{0,10},{1,11},{2,8},{3,9},{4,14},{5,15},{6,12},{7,13},{8,2},{9,3},... | collective-permute-start | bytes 688136 | tf_op jit(solution)/shard_map/ppermute | solution.py:284
  47.8 19.8 %collective-permute-start.13 = (bf16[576,256]{1,0:T(8,128)(2,1)S(1)}, bf16[576,256]{1,0:T(8,128)(2,1)S(1)}, u32[]{:S(2)}, u32[]{:S(2)}) collective-permute-start(bf16[576,256]{1,0:T(8,128)(2,1)S(1)} %copy-done.9), channel_id=1, source_target_pairs={{0,4},{1,5},{2,6},{3,7},{4,0},{5,1},{6,2},{7,3},{8,12},{9,13},{10,... | collective-permute-start | bytes 884744 | tf_op jit(solution)/shard_map/ppermute | solution.py:284
  47.8 38.9 %collective-permute-start.6 = (bf16[576,256]{1,0:T(8,128)(2,1)S(1)}, bf16[576,256]{1,0:T(8,128)(2,1)S(1)}, u32[]{:S(2)}, u32[]{:S(2)}) collective-permute-start(bf16[576,256]{1,0:T(8,128)(2,1)S(1)} %copy-done.8), channel_id=1, source_target_pairs={{0,5},{1,4},{2,7},{3,6},{4,1},{5,0},{6,3},{7,2},{8,13},{9,12},{10,... | collective-permute-start | bytes 884744 | tf_op jit(solution)/shard_map/ppermute | solution.py:284
  60.7 30.4 %collective-permute-start.4 = (bf16[576,256]{1,0:T(8,128)(2,1)S(1)}, bf16[576,256]{1,0:T(8,128)(2,1)S(1)}, u32[]{:S(2)}, u32[]{:S(2)}) collective-permute-start(bf16[576,256]{1,0:T(8,128)(2,1)S(1)} %copy-done.7), channel_id=1, source_target_pairs={{0,7},{1,6},{2,5},{3,4},{4,3},{5,2},{6,1},{7,0},{8,15},{9,14},{10,... | collective-permute-start | bytes 884744 | tf_op jit(solution)/shard_map/ppermute | solution.py:284
  65.6 38.9 %collective-permute-start.11 = (bf16[576,256]{1,0:T(8,128)(2,1)S(1)}, bf16[576,256]{1,0:T(8,128)(2,1)S(1)}, u32[]{:S(2)}, u32[]{:S(2)}) collective-permute-start(bf16[576,256]{1,0:T(8,128)(2,1)S(1)} %copy-done.6), channel_id=1, source_target_pairs={{0,6},{1,7},{2,4},{3,5},{4,2},{5,3},{6,0},{7,1},{8,14},{9,15},{10,... | collective-permute-start | bytes 884744 | tf_op jit(solution)/shard_map/ppermute | solution.py:284
  65.6 20.1 %collective-permute-start.8 = (bf16[448,256]{1,0:T(8,128)(2,1)}, bf16[448,256]{1,0:T(8,128)(2,1)S(1)}, u32[]{:S(2)}, u32[]{:S(2)}) collective-permute-start(bf16[448,256]{1,0:T(8,128)(2,1)} %get-tuple-element.57), channel_id=1, source_target_pairs={{0,12},{1,13},{2,14},{3,15},{4,8},{5,9},{6,10},{7,11},{8,4},{9,5},... | collective-permute-start | bytes 688136 | tf_op jit(solution)/shard_map/ppermute | solution.py:284
  67.6 38.0 %collective-permute-start.14 = (bf16[448,256]{1,0:T(8,128)(2,1)}, bf16[448,256]{1,0:T(8,128)(2,1)S(1)}, u32[]{:S(2)}, u32[]{:S(2)}) collective-permute-start(bf16[448,256]{1,0:T(8,128)(2,1)} %get-tuple-element.69), channel_id=1, source_target_pairs={{0,13},{1,12},{2,15},{3,14},{4,9},{5,8},{6,11},{7,10},{8,5},{9,4},... | collective-permute-start | bytes 688136 | tf_op jit(solution)/shard_map/ppermute | solution.py:284
  85.7 39.4 %collective-permute-start.9 = (bf16[576,256]{1,0:T(8,128)(2,1)S(1)}, bf16[576,256]{1,0:T(8,128)(2,1)S(1)}, u32[]{:S(2)}, u32[]{:S(2)}) collective-permute-start(bf16[576,256]{1,0:T(8,128)(2,1)S(1)} %copy-done.5), channel_id=1, source_target_pairs={{0,3},{1,2},{2,1},{3,0},{4,7},{5,6},{6,5},{7,4},{8,11},{9,10},{10,... | collective-permute-start | bytes 884744 | tf_op jit(solution)/shard_map/ppermute | solution.py:284
  86.7 38.4 %collective-permute-start.7 = (bf16[448,256]{1,0:T(8,128)(2,1)}, bf16[448,256]{1,0:T(8,128)(2,1)S(1)}, u32[]{:S(2)}, u32[]{:S(2)}) collective-permute-start(bf16[448,256]{1,0:T(8,128)(2,1)} %get-tuple-element.54), channel_id=1, source_target_pairs={{0,14},{1,15},{2,12},{3,13},{4,10},{5,11},{6,8},{7,9},{8,6},{9,7},... | collective-permute-start | bytes 688136 | tf_op jit(solution)/shard_map/ppermute | solution.py:284
  91.1 36.6 %collective-permute-start.5 = (bf16[448,256]{1,0:T(8,128)(2,1)}, bf16[448,256]{1,0:T(8,128)(2,1)S(1)}, u32[]{:S(2)}, u32[]{:S(2)}) collective-permute-start(bf16[448,256]{1,0:T(8,128)(2,1)} %get-tuple-element.50), channel_id=1, source_target_pairs={{0,15},{1,14},{2,13},{3,12},{4,11},{5,10},{6,9},{7,8},{8,7},{9,6},... | collective-permute-start | bytes 688136 | tf_op jit(solution)/shard_map/ppermute | solution.py:284
  104.5 20.6 %collective-permute-start.12 = (bf16[576,256]{1,0:T(8,128)(2,1)S(1)}, bf16[576,256]{1,0:T(8,128)(2,1)S(1)}, u32[]{:S(2)}, u32[]{:S(2)}) collective-permute-start(bf16[576,256]{1,0:T(8,128)(2,1)S(1)} %copy-done.4), channel_id=1, source_target_pairs={{0,2},{1,3},{2,0},{3,1},{4,6},{5,7},{6,4},{7,5},{8,10},{9,11},{10,... | collective-permute-start | bytes 884744 | tf_op jit(solution)/shard_map/ppermute | solution.py:284
  105.6 14.7 %copy-start = (bf16[576,256]{1,0:T(8,128)(2,1)S(1)}, bf16[576,256]{1,0:T(8,128)(2,1)}, u32[]{:S(2)}) copy-start(bf16[576,256]{1,0:T(8,128)(2,1)} %get-tuple-element.43.refs_22_) | copy-start | bytes 884740
  105.6 19.6 %collective-permute-start.15 = (bf16[576,256]{1,0:T(8,128)(2,1)S(1)}, bf16[576,256]{1,0:T(8,128)(2,1)S(1)}, u32[]{:S(2)}, u32[]{:S(2)}) collective-permute-start(bf16[576,256]{1,0:T(8,128)(2,1)S(1)} %copy-done.3), channel_id=1, source_target_pairs={{0,1},{1,0},{2,3},{3,2},{4,5},{5,4},{6,7},{7,6},{8,9},{9,8},{10,11... | collective-permute-start | bytes 884744 | tf_op jit(solution)/shard_map/ppermute | solution.py:284
where the time goes:
time: 130 us
  waiting for transfers between devices  60.5 us (47%)
  Pallas kernels  35.3 us (27%)
  starting transfers between devices  29 us (22%)
  local copies, waits for them, and re-layouts  3.6 us (3%)
  other arithmetic  1.36 us (1%)
    ppermute x16, waiting for transfers between devices, swap(): return lax.ppermute(values, 'docs', [(i, i ^ k) for i in range(devices)])  53.5 us
    ppermute x16, starting transfers between devices, swap(): return lax.ppermute(values, 'docs', [(i, i ^ k) for i in range(devices)])  22.1 us
    pallas_call x1, Pallas kernels, precondition(): call(kernel, jax.ShapeDtypeStruct(queries.shape, queries.dtype), (total /...  13.1 us
    pallas_call x3, Pallas kernels, gather_pieces(): call(kernel, [pltpu.HBM((features, entries), tables[0][0].dtype)] * count...  12.7 us
    pallas_call x3, Pallas kernels, score_pieces(): call(kernel, jax.ShapeDtypeStruct((queries, entries), jnp.float32), (1,),...  9.5 us
    all_to_all x1, waiting for transfers between devices, on_device(): lax.all_to_all(jnp.broadcast_to(own_ids, (devices, 1, entries)), 'docs',...  7.03 us
    all_to_all x1, starting transfers between devices, on_device(): lax.all_to_all(jnp.broadcast_to(own_ids, (devices, 1, entries)), 'docs',...  6.9 us
    unnamed x21, local copies, waits for them, and re-layouts  2.97 us
  transfers between devices with their start and end apart: 17, of which 6 were waited for; matrix products, arithmetic and copies ran while one was open for 2% of the time, Pallas kernels for 24%

commit v1 on v0

--- a/solution.py
+++ b/solution.py
@@ -37,6 +37,38 @@
     return jnp.concatenate(
         [in_group * (group == g).astype(jnp.bfloat16) for g in range(docs // LANES)], axis=0
     )
+
+
+def prepare(doc_grads, owners, rows, devices, tail):
+    docs, width = doc_grads.shape
+    entries = rows.shape[0]
+    doc_count = docs // devices
+    block = max(tail, LANES)
+
+    def kernel(docs_ref, owners_ref, rows_ref, tail_ref, ids_ref):
+        tail_ref[...] = docs_ref[...].T[block - tail :, :]
+        ids = owners_ref[...] * doc_count + rows_ref[...]
+        ids_ref[...] = jnp.broadcast_to(ids[None], ids_ref.shape)
+
+    return call(
+        kernel,
+        [
+            pltpu.HBM((tail, docs), doc_grads.dtype),
+            pltpu.HBM((devices, 1, entries), jnp.int32),
+        ],
+        (1,),
+        [
+            pl.BlockSpec((docs, block), lambda i: (0, width // block - 1)),
+            pl.BlockSpec((1, entries), lambda i: (0, 0)),
+            pl.BlockSpec((1, entries), lambda i: (0, 0)),
+        ],
+        [
+            pl.BlockSpec((tail, docs), lambda i: (0, 0)),
+            pl.BlockSpec((devices, 1, entries), lambda i: (0, 0, 0)),
+        ],
+        0,
+        2 * docs * (block + tail),
+    )(doc_grads, owners.reshape(1, entries), rows.reshape(1, entries))
 
 
 def gather_rows(base, ids, tables, count):
@@ -283,60 +315,61 @@
     def swap(values, k):
         return lax.ppermute(values, "docs", [(i, i ^ k) for i in range(devices)])
 
+    def exchange(values):
+        return lax.all_to_all(values, "docs", split_axis=0, concat_axis=0, tiled=True)
+
     tail = width // 8 if width % (4 * LANES) == 0 else 0
-    table = doc_grads.T
-    if tail:
-        across = swap(table[width - tail :], half)
-    own_ids = cand_owner[:, 0] * doc_count + cand_row
-    ids = lax.all_to_all(
-        jnp.broadcast_to(own_ids, (devices, 1, entries)), "docs", split_axis=0, concat_axis=0, tiled=True
-    )
     if not tail:
-        picked = gather_rows(jnp.zeros((1,), jnp.int32), ids, [table], devices)
-        chosen = lax.all_to_all(picked, "docs", split_axis=0, concat_axis=0, tiled=True)
-        return score_all(precondition(query_grads, left_inv, right_inv), chosen, scale)
-
-    first, flight = 2, 5
-    far = list(range(half, devices))
-    near = [*range(half // 2, half), *range(half // 2 - 1, 0, -1)]
+        own_ids = cand_owner[:, 0] * doc_count + cand_row
+        ids = exchange(jnp.broadcast_to(own_ids, (devices, 1, entries)))
+        picked = gather_rows(jnp.zeros((1,), jnp.int32), ids, [doc_grads.T], devices)
+        return score_all(precondition(query_grads, left_inv, right_inv), exchange(picked), scale)
+
+    own_tail, own_ids = prepare(doc_grads, cand_owner, cand_row, devices, tail)
+    across = swap(own_tail, half)
+    ids = exchange(own_ids)
+    table = after(doc_grads, own_ids).T
+    far, near = list(range(half, devices)), list(range(1, half))
     inside = [0, *near]
     body = [(table, width - tail)]
-    order = far[:first]
-    rest = [far[first:-1], list(near)]
-    while any(rest):
-        order += [part.pop(0) for part in rest if part]
-    order.append(far[-1])
     ids = after(ids, across)
-    pieces = dict(zip(far, gather_pieces(me, ids, body, far[:first])))
-    ids = after(ids, pieces[order[0]])
+    pieces = dict(zip(far, gather_pieces(me, ids, body, far[:2])))
+    ids = after(ids, pieces[far[0]])
     pieces.update(zip(inside, gather_pieces(me, ids, [(table, width), (across, tail)], inside)))
     ids = after(ids, pieces[0])
-    pieces.update(zip(far[first:], gather_pieces(me, ids, body, far[first:])))
-    came = {0: pieces[0]}
-    for position, k in enumerate(order):
-        piece = pieces[k]
-        if position >= first:
-            before = [came[j] for j in order[:first]]
-            if position >= flight + first:
-                before = [came[order[position - flight]]]
-            piece = after(piece, *before)
-        came[k] = swap(piece, k)
-    prepared = precondition(after(query_grads, came[order[first - 1]]), left_inv, right_inv)
-
-    total = None
-    stops = [0, len(order) - 5, len(order) - 1, len(order)]
-    for start, stop in zip(stops, stops[1:]):
-        keys = [*([0] if start == 0 else []), *order[start:stop]]
-        total = score_pieces(
-            me,
-            prepared,
-            {k: came[k] for k in keys if k >= half},
-            {k: came[k] for k in keys if k < half},
-            total,
-            width,
-            half,
-            scale if stop == len(order) else 1.0,
-        )
+    pieces.update(zip(far[2:], gather_pieces(me, ids, body, far[2:])))
+    near = [half // 2, *near[1 : half // 2 - 1], *near[half // 2 :], 1]
+    counts = [(2, 0), (2, 3)]
+    phases = []
+    while far or near:
+        fars, nears = counts.pop(0) if counts else (3, 2)
+        phases.append(far[:fars] + near[:nears])
+        far, near = far[fars:], near[nears:]
+
+    prepared = total = None
+    came, ready, waiting = {0: pieces[0]}, [], [0]
+    for number, phase in enumerate(phases):
+        for k in phase:
+            came[k] = swap(after(pieces[k], *ready) if ready else pieces[k], k)
+        ready = [came[k] for k in phase]
+        if number == 0:
+            prepared = precondition(after(query_grads, *ready), left_inv, right_inv)
+        if number == 1:
+            ready.append(prepared)
+        waiting += phase
+        last = number == len(phases) - 1
+        if last or number == len(phases) - 2:
+            total = score_pieces(
+                me,
+                prepared,
+                {k: came[k] for k in waiting if k >= half},
+                {k: came[k] for k in waiting if k < half},
+                total,
+                width,
+                half,
+                scale if last else 1.0,
+            )
+            waiting = []
     return total
 
 

time: 130 us -> 132 us (1.015)
  the two profiles are of different devices: /device:TPU:25 before, /device:TPU:0 now
where the time goes in v1:
time: 132 us; the launch traced here: 131 us
  waiting for transfers between devices  54.6 us (41%)
  starting transfers between devices  35.5 us (27%)
  Pallas kernels  35.1 us (27%)
  local copies, waits for them, and re-layouts  5.94 us (4%)
    ppermute x16, waiting for transfers between devices, swap(): return lax.ppermute(values, 'docs', [(i, i ^ k) for i in range(devices)])  48 us
    ppermute x16, starting transfers between devices, swap(): return lax.ppermute(values, 'docs', [(i, i ^ k) for i in range(devices)])  31.6 us
    pallas_call x1, Pallas kernels, precondition(): call(kernel, jax.ShapeDtypeStruct(queries.shape, queries.dtype), (total /...  13.1 us
    pallas_call x3, Pallas kernels, gather_pieces(): call(kernel, [pltpu.HBM((features, entries), tables[0][0].dtype)] * count...  12.6 us
    pallas_call x2, Pallas kernels, score_pieces(): call(kernel, jax.ShapeDtypeStruct((queries, entries), jnp.float32), (1,),...  8.46 us
    all_to_all x1, waiting for transfers between devices, exchange(): lax.all_to_all(values, 'docs', split_axis=0, concat_axis=0, tiled=True)  6.54 us
    all_to_all x1, starting transfers between devices, exchange(): lax.all_to_all(values, 'docs', split_axis=0, concat_axis=0, tiled=True)  3.91 us
    unnamed x34, local copies, waits for them, and re-layouts  3.01 us
  transfers between devices with their start and end apart: 17, of which 8 were waited for; matrix products, arithmetic and copies ran while one was open for 2% of the time, Pallas kernels for 22%

profile of v1, /device:TPU:0, one launch (start us, length us, event | category | flops | bytes accessed | tf_op | source)
XLA Modules:
  0.0 131.2 jit_solution(6017402095144392866)
XLA Ops:
  0.0 1.6 %copy-done = bf16[2048,512]{1,0:T(8,128)(2,1)S(1)} copy-done((bf16[2048,512]{1,0:T(8,128)(2,1)S(1)}, bf16[2048,512]{1,0:T(8,128)(2,1)}, u32[]{:S(2)}) %copy-start) | copy-done | bytes 2097176
  1.6 0.7 copy-done.4
  2.3 0.7 copy-done.5
  3.0 0.9 shard_map.64
  3.9 4.0 %collective-permute-start = (bf16[64,2048]{1,0:T(8,128)(2,1)}, bf16[64,2048]{1,0:T(8,128)(2,1)S(1)}, u32[]{:S(2)}, u32[]{:S(2)}) collective-permute-start(bf16[64,2048]{1,0:T(8,128)(2,1)} %get-tuple-element.42), channel_id=1, source_target_pairs={{0,8},{1,9},{2,10},{3,11},{4,12},{5,13},{6,14},{7,15},{8,0},{9,1},... | collective-permute-start | bytes 786440 | tf_op jit(solution)/shard_map/ppermute | solution.py:316
  7.9 3.9 %all-to-all-start = ((s32[16,1,256]{2,1,0:T(1,128)}), s32[16,1,256]{2,1,0:T(1,128)S(1)}, u32[]{:S(2)}, u32[]{:S(2)}) async-start(s32[16,1,256]{2,1,0:T(1,128)} %get-tuple-element.41), calls=%async_computation | async-start | bytes 32768 | tf_op jit(solution)/shard_map/all_to_all | solution.py:319
  11.8 2.9 %copy.7 = bf16[2048,512]{0,1:T(8,128)(2,1)S(1)} copy(bf16[2048,512]{1,0:T(8,128)(2,1)} %docs_ref.1) | data formatting | bytes 4194304 | tf_op jit(solution)/shard_map/optimization_barrier | solution.py:302
  14.8 6.5 %all-to-all-done.refs_0_.refs_1_.refs_2_.refs_3_.refs_4_.refs_5_.refs_6_.refs_7_ = s32[16,1,256]{2,1,0:T(1,128)S(1)} async-done(((s32[16,1,256]{2,1,0:T(1,128)}), s32[16,1,256]{2,1,0:T(1,128)S(1)}, u32[]{:S(2)}, u32[]{:S(2)}) %all-to-all-start) | async-done | bytes 16416 | tf_op jit(solution)/shard_map/all_to_all | solution.py:319
  21.3 0.0 collective-permute-done.refs_9_
  21.3 1.9 %shard_map.65 = (bf16[448,256]{1,0:T(8,128)(2,1)}, bf16[448,256]{1,0:T(8,128)(2,1)}) custom-call(s32[1]{0:T(128)} %bitcast.me_ref, s32[16,1,256]{2,1,0:T(1,128)S(1)} %all-to-all-done.refs_0_.refs_1_.refs_2_.refs_3_.refs_4_.refs_5_.refs_6_.refs_7_, s32[16,1,256]{2,1,0:T(1,128)S(1)} %all-to-all-done.refs_0_.refs_1_.refs_2_.refs_3_.refs_4_.refs_5_.refs_6_.refs_7_, ...), custom_call_target="tpu_custom_call" | custom-call | flops 939524096 | bytes 2293760 | tf_op jit(solution)/shard_map/pallas_call | solution.py:117
  23.2 2.7 %collective-permute-start.1 = (bf16[448,256]{1,0:T(8,128)(2,1)}, bf16[448,256]{1,0:T(8,128)(2,1)S(1)}, u32[]{:S(2)}, u32[]{:S(2)}) collective-permute-start(bf16[448,256]{1,0:T(8,128)(2,1)} %get-tuple-element.45), channel_id=1, source_target_pairs={{0,8},{1,9},{2,10},{3,11},{4,12},{5,13},{6,14},{7,15},{8,0},{9,1},... | collective-permute-start | bytes 688136 | tf_op jit(solution)/shard_map/ppermute | solution.py:316
  25.9 0.0 collective-permute-start.2
  25.9 6.9 %shard_map.67 = (bf16[576,256]{1,0:T(8,128)(2,1)}, bf16[576,256]{1,0:T(8,128)(2,1)}, bf16[576,256]{1,0:T(8,128)(2,1)}, bf16[576,256]{1,0:T(8,128)(2,1)}, bf16[57...) custom-call(s32[1]{0:T(128)} %bitcast.me_ref, ...), custom_call_target="tpu_custom_call" | custom-call | flops 4831838208 | bytes 4718592 | tf_op jit(solution)/shard_map/pallas_call | solution.py:117
  32.7 0.0 copy-start.2
  32.8 0.0 copy-start.3
  32.8 3.8 %shard_map.68 = (bf16[448,256]{1,0:T(8,128)(2,1)}, bf16[448,256]{1,0:T(8,128)(2,1)}, bf16[448,256]{1,0:T(8,128)(2,1)}, bf16[448,256]{1,0:T(8,128)(2,1)}, bf16[44...) custom-call(s32[1]{0:T(128)} %bitcast.me_ref, ...), custom_call_target="tpu_custom_call" | custom-call | flops 2818572288 | bytes 3211264 | tf_op jit(solution)/shard_map/pallas_call | solution.py:117
  36.6 9.2 %collective-permute-done.2.refs_20_ = bf16[448,256]{1,0:T(8,128)(2,1)S(1)} collective-permute-done((bf16[448,256]{1,0:T(8,128)(2,1)}, bf16[448,256]{1,0:T(8,128)(2,1)S(1)}, u32[]{:S(2)}, u32[]{:S(2)}) %collective-permute-start.2) | collective-permute-done | bytes 229408 | tf_op jit(solution)/shard_map/ppermute | solution.py:316
  45.9 0.0 collective-permute-done.1.refs_19_
  45.9 0.0 copy-start.15
  45.9 0.0 copy-start.14
  45.9 0.0 copy-start.7
  45.9 0.0 copy-start.6
  45.9 0.0 copy-start.13
  45.9 0.0 copy-start.1
  45.9 0.1 collective-permute-start.4
  46.0 4.1 %collective-permute-start.3 = (bf16[448,256]{1,0:T(8,128)(2,1)}, bf16[448,256]{1,0:T(8,128)(2,1)S(1)}, u32[]{:S(2)}, u32[]{:S(2)}) collective-permute-start(bf16[448,256]{1,0:T(8,128)(2,1)} %get-tuple-element.54), channel_id=1, source_target_pairs={{0,10},{1,11},{2,8},{3,9},{4,14},{5,15},{6,12},{7,13},{8,2},{9,3},... | collective-permute-start | bytes 688136 | tf_op jit(solution)/shard_map/ppermute | solution.py:316
  50.1 0.0 copy-done.12
  50.1 0.0 collective-permute-start.7
  50.1 0.0 copy-done.11
  50.1 1.2 collective-permute-start.6
  51.3 0.0 copy-done.10
  51.3 1.5 %collective-permute-start.5 = (bf16[576,256]{1,0:T(8,128)(2,1)S(1)}, bf16[576,256]{1,0:T(8,128)(2,1)S(1)}, u32[]{:S(2)}, u32[]{:S(2)}) collective-permute-start(bf16[576,256]{1,0:T(8,128)(2,1)S(1)} %copy-done.10), channel_id=1, source_target_pairs={{0,4},{1,5},{2,6},{3,7},{4,0},{5,1},{6,2},{7,3},{8,12},{9,13},{10,... | collective-permute-start | bytes 884744 | tf_op jit(solution)/shard_map/ppermute | solution.py:316
  52.8 0.0 copy-done.2
  52.8 0.0 copy-done.3
  52.8 13.1 %shard_map.66.refs_0_.refs_1_.refs_2_.refs_3_.refs_4_.refs_5_.refs_6_.refs_7_.refs_8_.refs_9_.refs_10_.refs_11_.refs_12_.refs_13_.refs_14_.refs_15_.refs_16_.refs_17_.refs_18_ = bf16[512,8192]{1,0:T(8,128)(2,1)} custom-call(bf16[512,8192]{1,0:T(8,128)(2,1)} %queries_ref, bf16[2,32,32]{2,1,0:T(8,128)(2,1)S(1)} %copy-done.3, bf16[2,128,128]{2,1,0:T(8,128)(2,1)S(1)} %copy-done.2), custom_call_target="tpu_custom_call" | custom-call | flops 4294967296 | bytes 16777216 | tf_op jit(solution)/shard_map/pallas_call | solution.py:281
  65.9 0.0 collective-permute-done.4.refs_22_
  65.9 4.9 %collective-permute-done.3.refs_21_ = bf16[448,256]{1,0:T(8,128)(2,1)S(1)} collective-permute-done((bf16[448,256]{1,0:T(8,128)(2,1)}, bf16[448,256]{1,0:T(8,128)(2,1)S(1)}, u32[]{:S(2)}, u32[]{:S(2)}) %collective-permute-start.3) | collective-permute-done | bytes 229408 | tf_op jit(solution)/shard_map/ppermute | solution.py:316
  70.8 0.0 collective-permute-done.7.refs_29_
  70.8 3.3 %collective-permute-done.6.refs_28_ = bf16[576,256]{1,0:T(8,128)(2,1)S(1)} collective-permute-done((bf16[576,256]{1,0:T(8,128)(2,1)S(1)}, bf16[576,256]{1,0:T(8,128)(2,1)S(1)}, u32[]{:S(2)}, u32[]{:S(2)}) %collective-permute-start.6) | collective-permute-done | bytes 294944 | tf_op jit(solution)/shard_map/ppermute | solution.py:316
  74.0 0.0 collective-permute-done.5.refs_27_
  74.0 0.0 copy-done.9
  74.0 0.7 collective-permute-start.11
  74.8 0.0 copy-done.8
  74.8 1.2 collective-permute-start.12
  75.9 0.0 copy-done.16
  76.0 4.6 %collective-permute-start.8 = (bf16[448,256]{1,0:T(8,128)(2,1)S(1)}, bf16[448,256]{1,0:T(8,128)(2,1)S(1)}, u32[]{:S(2)}, u32[]{:S(2)}) collective-permute-start(bf16[448,256]{1,0:T(8,128)(2,1)S(1)} %copy-done.16), channel_id=1, source_target_pairs={{0,12},{1,13},{2,14},{3,15},{4,8},{5,9},{6,10},{7,11},{8,4},{9,5},... | collective-permute-start | bytes 688136 | tf_op jit(solution)/shard_map/ppermute | solution.py:316
  80.6 0.0 copy-done.15
  80.6 0.1 collective-permute-start.9
  80.7 0.0 copy-done.14
  80.7 4.3 %collective-permute-start.10 = (bf16[448,256]{1,0:T(8,128)(2,1)S(1)}, bf16[448,256]{1,0:T(8,128)(2,1)S(1)}, u32[]{:S(2)}, u32[]{:S(2)}) collective-permute-start(bf16[448,256]{1,0:T(8,128)(2,1)S(1)} %copy-done.14), channel_id=1, source_target_pairs={{0,14},{1,15},{2,12},{3,13},{4,10},{5,11},{6,8},{7,9},{8,6},{9,7},... | collective-permute-start | bytes 688136 | tf_op jit(solution)/shard_map/ppermute | solution.py:316
  85.0 13.3 %collective-permute-done.8.refs_23_ = bf16[448,256]{1,0:T(8,128)(2,1)S(1)} collective-permute-done((bf16[448,256]{1,0:T(8,128)(2,1)S(1)}, bf16[448,256]{1,0:T(8,128)(2,1)S(1)}, u32[]{:S(2)}, u32[]{:S(2)}) %collective-permute-start.8) | collective-permute-done | bytes 229408 | tf_op jit(solution)/shard_map/ppermute | solution.py:316
  98.2 3.1 %collective-permute-done.9.refs_24_ = bf16[448,256]{1,0:T(8,128)(2,1)S(1)} collective-permute-done((bf16[448,256]{1,0:T(8,128)(2,1)S(1)}, bf16[448,256]{1,0:T(8,128)(2,1)S(1)}, u32[]{:S(2)}, u32[]{:S(2)}) %collective-permute-start.9) | collective-permute-done | bytes 229408 | tf_op jit(solution)/shard_map/ppermute | solution.py:316
  101.4 5.9 %collective-permute-done.10.refs_25_ = bf16[448,256]{1,0:T(8,128)(2,1)S(1)} collective-permute-done((bf16[448,256]{1,0:T(8,128)(2,1)S(1)}, bf16[448,256]{1,0:T(8,128)(2,1)S(1)}, u32[]{:S(2)}, u32[]{:S(2)}) %collective-permute-start.10) | collective-permute-done | bytes 229408 | tf_op jit(solution)/shard_map/ppermute | solution.py:316
  107.3 0.0 collective-permute-done.11.refs_30_
  107.3 0.0 collective-permute-done.12.refs_31_
  107.3 0.0 copy-done.7
  107.3 3.4 %collective-permute-start.14 = (bf16[576,256]{1,0:T(8,128)(2,1)S(1)}, bf16[576,256]{1,0:T(8,128)(2,1)S(1)}, u32[]{:S(2)}, u32[]{:S(2)}) collective-permute-start(bf16[576,256]{1,0:T(8,128)(2,1)S(1)} %copy-done.7), channel_id=1, source_target_pairs={{0,7},{1,6},{2,5},{3,4},{4,3},{5,2},{6,1},{7,0},{8,15},{9,14},{10,... | collective-permute-start | bytes 884744 | tf_op jit(solution)/shard_map/ppermute | solution.py:316
  110.8 1.0 collective-permute-start.15
  111.8 2.6 %collective-permute-start.13 = (bf16[448,256]{1,0:T(8,128)(2,1)S(1)}, bf16[448,256]{1,0:T(8,128)(2,1)S(1)}, u32[]{:S(2)}, u32[]{:S(2)}) collective-permute-start(bf16[448,256]{1,0:T(8,128)(2,1)S(1)} %copy-done.13), channel_id=1, source_target_pairs={{0,15},{1,14},{2,13},{3,12},{4,11},{5,10},{6,9},{7,8},{8,7},{9,6},... | collective-permute-start | bytes 688136 | tf_op jit(solution)/shard_map/ppermute | solution.py:316
  114.4 5.5 %shard_map.69.refs_8_ = f32[512,256]{1,0:T(8,128)S(1)} custom-call(s32[1]{0:T(128)} %bitcast.me_ref, bf16[512,8192]{1,0:T(8,128)(2,1)} %shard_map.66.refs_0_.refs_1_.refs_2_.refs_3_.refs_4_.refs_5_.refs_6_.refs_7_.refs_8_.refs_9_.refs_10_.refs_11_.refs_12_.refs_13_.refs_14_.refs_15_.refs_16_.refs_17_.refs_18_, ...), custom_call_target="tpu_custom_call" | custom-call | flops 1728053248 | bytes 11173888 | tf_op jit(solution)/shard_map/pallas_call | solution.py:172
  119.9 8.3 %collective-permute-done.13.refs_5_ = bf16[448,256]{1,0:T(8,128)(2,1)S(1)} collective-permute-done((bf16[448,256]{1,0:T(8,128)(2,1)S(1)}, bf16[448,256]{1,0:T(8,128)(2,1)S(1)}, u32[]{:S(2)}, u32[]{:S(2)}) %collective-permute-start.13) | collective-permute-done | bytes 229408 | tf_op jit(solution)/shard_map/ppermute | solution.py:316
  128.2 0.0 collective-permute-done.14.refs_6_
  128.2 0.0 collective-permute-done.15.refs_7_
  128.2 3.0 %shard_map.70 = f32[512,256]{1,0:T(8,128)} custom-call(s32[1]{0:T(128)} %bitcast.me_ref, bf16[512,8192]{1,0:T(8,128)(2,1)} %shard_map.66.refs_0_.refs_1_.refs_2_.refs_3_.refs_4_.refs_5_.refs_6_.refs_7_.refs_8_.refs_9_.refs_10_.refs_11_.refs_12_.refs_13_.refs_14_.refs_15_.refs_16_.refs_17_.refs_18_, ...), custom_call_target="tpu_custom_call" | custom-call | flops 419430400 | bytes 3506176 | tf_op jit(solution)/shard_map/pallas_call | solution.py:172
  (12 shorter events, 0.0 us)
Async XLA Ops:
  0.0 1.6 %copy-start = (bf16[2048,512]{1,0:T(8,128)(2,1)S(1)}, bf16[2048,512]{1,0:T(8,128)(2,1)}, u32[]{:S(2)}) copy-start(bf16[2048,512]{1,0:T(8,128)(2,1)} %docs_ref.1) | copy-start | bytes 6291460
  1.6 0.7 copy-start.4
  2.3 0.7 copy-start.5
  3.9 17.4 %collective-permute-start = (bf16[64,2048]{1,0:T(8,128)(2,1)}, bf16[64,2048]{1,0:T(8,128)(2,1)S(1)}, u32[]{:S(2)}, u32[]{:S(2)}) collective-permute-start(bf16[64,2048]{1,0:T(8,128)(2,1)} %get-tuple-element.42), channel_id=1, source_target_pairs={{0,8},{1,9},{2,10},{3,11},{4,12},{5,13},{6,14},{7,15},{8,0},{9,1},... | collective-permute-start | bytes 786440 | tf_op jit(solution)/shard_map/ppermute | solution.py:316
  7.9 13.4 %all-to-all-start = ((s32[16,1,256]{2,1,0:T(1,128)}), s32[16,1,256]{2,1,0:T(1,128)S(1)}, u32[]{:S(2)}, u32[]{:S(2)}) async-start(s32[16,1,256]{2,1,0:T(1,128)} %get-tuple-element.41), calls=%async_computation | async-start | bytes 32768 | tf_op jit(solution)/shard_map/all_to_all | solution.py:319
  23.2 22.6 %collective-permute-start.1 = (bf16[448,256]{1,0:T(8,128)(2,1)}, bf16[448,256]{1,0:T(8,128)(2,1)S(1)}, u32[]{:S(2)}, u32[]{:S(2)}) collective-permute-start(bf16[448,256]{1,0:T(8,128)(2,1)} %get-tuple-element.45), channel_id=1, source_target_pairs={{0,8},{1,9},{2,10},{3,11},{4,12},{5,13},{6,14},{7,15},{8,0},{9,1},... | collective-permute-start | bytes 688136 | tf_op jit(solution)/shard_map/ppermute | solution.py:316
  25.9 20.0 %collective-permute-start.2 = (bf16[448,256]{1,0:T(8,128)(2,1)}, bf16[448,256]{1,0:T(8,128)(2,1)S(1)}, u32[]{:S(2)}, u32[]{:S(2)}) collective-permute-start(bf16[448,256]{1,0:T(8,128)(2,1)} %get-tuple-element.46), channel_id=1, source_target_pairs={{0,9},{1,8},{2,11},{3,10},{4,13},{5,12},{6,15},{7,14},{8,1},{9,0},... | collective-permute-start | bytes 688136 | tf_op jit(solution)/shard_map/ppermute | solution.py:316
  32.7 17.3 %copy-start.12 = (bf16[576,256]{1,0:T(8,128)(2,1)S(1)}, bf16[576,256]{1,0:T(8,128)(2,1)}, u32[]{:S(2)}) copy-start(bf16[576,256]{1,0:T(8,128)(2,1)} %get-tuple-element.62) | copy-start | bytes 884740
  32.7 17.3 %copy-start.11 = (bf16[576,256]{1,0:T(8,128)(2,1)S(1)}, bf16[576,256]{1,0:T(8,128)(2,1)}, u32[]{:S(2)}) copy-start(bf16[576,256]{1,0:T(8,128)(2,1)} %get-tuple-element.60) | copy-start | bytes 884740
  32.7 18.6 %copy-start.10 = (bf16[576,256]{1,0:T(8,128)(2,1)S(1)}, bf16[576,256]{1,0:T(8,128)(2,1)}, u32[]{:S(2)}) copy-start(bf16[576,256]{1,0:T(8,128)(2,1)} %get-tuple-element.58) | copy-start | bytes 884740
  32.7 20.0 %copy-start.2 = (bf16[2,128,128]{2,1,0:T(8,128)(2,1)S(1)}, bf16[2,128,128]{2,1,0:T(8,128)(2,1)}, u32[]{:S(2)}) copy-start(bf16[2,128,128]{2,1,0:T(8,128)(2,1)} %right_inv_ref.1) | copy-start | bytes 196612
  32.8 20.0 %copy-start.3 = (bf16[2,32,32]{2,1,0:T(8,128)(2,1)S(1)}, bf16[2,32,32]{2,1,0:T(8,128)(2,1)}, u32[]{:S(2)}) copy-start(bf16[2,32,32]{2,1,0:T(8,128)(2,1)} %left_inv_ref.1) | copy-start | bytes 12292
  45.9 28.2 %copy-start.9 = (bf16[576,256]{1,0:T(8,128)(2,1)S(1)}, bf16[576,256]{1,0:T(8,128)(2,1)}, u32[]{:S(2)}) copy-start(bf16[576,256]{1,0:T(8,128)(2,1)} %get-tuple-element.69) | copy-start | bytes 884740
  45.9 28.9 %copy-start.8 = (bf16[576,256]{1,0:T(8,128)(2,1)S(1)}, bf16[576,256]{1,0:T(8,128)(2,1)}, u32[]{:S(2)}) copy-start(bf16[576,256]{1,0:T(8,128)(2,1)} %get-tuple-element.71) | copy-start | bytes 884740
  45.9 30.1 %copy-start.16 = (bf16[448,256]{1,0:T(8,128)(2,1)S(1)}, bf16[448,256]{1,0:T(8,128)(2,1)}, u32[]{:S(2)}) copy-start(bf16[448,256]{1,0:T(8,128)(2,1)} %get-tuple-element.63) | copy-start | bytes 688132
  45.9 34.7 %copy-start.15 = (bf16[448,256]{1,0:T(8,128)(2,1)S(1)}, bf16[448,256]{1,0:T(8,128)(2,1)}, u32[]{:S(2)}) copy-start(bf16[448,256]{1,0:T(8,128)(2,1)} %get-tuple-element.65) | copy-start | bytes 688132
  45.9 34.8 %copy-start.14 = (bf16[448,256]{1,0:T(8,128)(2,1)S(1)}, bf16[448,256]{1,0:T(8,128)(2,1)}, u32[]{:S(2)}) copy-start(bf16[448,256]{1,0:T(8,128)(2,1)} %get-tuple-element.67) | copy-start | bytes 688132
  45.9 61.4 %copy-start.7 = (bf16[576,256]{1,0:T(8,128)(2,1)S(1)}, bf16[576,256]{1,0:T(8,128)(2,1)}, u32[]{:S(2)}) copy-start(bf16[576,256]{1,0:T(8,128)(2,1)} %get-tuple-element.74) | copy-start | bytes 884740
  45.9 64.9 %copy-start.6 = (bf16[576,256]{1,0:T(8,128)(2,1)S(1)}, bf16[576,256]{1,0:T(8,128)(2,1)}, u32[]{:S(2)}) copy-start(bf16[576,256]{1,0:T(8,128)(2,1)} %get-tuple-element.76) | copy-start | bytes 884740
  45.9 65.9 %copy-start.13 = (bf16[448,256]{1,0:T(8,128)(2,1)S(1)}, bf16[448,256]{1,0:T(8,128)(2,1)}, u32[]{:S(2)}) copy-start(bf16[448,256]{1,0:T(8,128)(2,1)} %get-tuple-element.72) | copy-start | bytes 688132
  45.9 68.5 %copy-start.1 = (bf16[576,256]{1,0:T(8,128)(2,1)S(1)}, bf16[576,256]{1,0:T(8,128)(2,1)}, u32[]{:S(2)}) copy-start(bf16[576,256]{1,0:T(8,128)(2,1)} %get-tuple-element.49.refs_26_) | copy-start | bytes 884740
  45.9 20.0 %collective-permute-start.4 = (bf16[448,256]{1,0:T(8,128)(2,1)}, bf16[448,256]{1,0:T(8,128)(2,1)S(1)}, u32[]{:S(2)}, u32[]{:S(2)}) collective-permute-start(bf16[448,256]{1,0:T(8,128)(2,1)} %get-tuple-element.56), channel_id=1, source_target_pairs={{0,11},{1,10},{2,9},{3,8},{4,15},{5,14},{6,13},{7,12},{8,3},{9,2},... | collective-permute-start | bytes 688136 | tf_op jit(solution)/shard_map/ppermute | solution.py:316
  46.0 24.8 %collective-permute-start.3 = (bf16[448,256]{1,0:T(8,128)(2,1)}, bf16[448,256]{1,0:T(8,128)(2,1)S(1)}, u32[]{:S(2)}, u32[]{:S(2)}) collective-permute-start(bf16[448,256]{1,0:T(8,128)(2,1)} %get-tuple-element.54), channel_id=1, source_target_pairs={{0,10},{1,11},{2,8},{3,9},{4,14},{5,15},{6,12},{7,13},{8,2},{9,3},... | collective-permute-start | bytes 688136 | tf_op jit(solution)/shard_map/ppermute | solution.py:316
  50.1 20.7 %collective-permute-start.7 = (bf16[576,256]{1,0:T(8,128)(2,1)S(1)}, bf16[576,256]{1,0:T(8,128)(2,1)S(1)}, u32[]{:S(2)}, u32[]{:S(2)}) collective-permute-start(bf16[576,256]{1,0:T(8,128)(2,1)S(1)} %copy-done.12), channel_id=1, source_target_pairs={{0,3},{1,2},{2,1},{3,0},{4,7},{5,6},{6,5},{7,4},{8,11},{9,10},{10,... | collective-permute-start | bytes 884744 | tf_op jit(solution)/shard_map/ppermute | solution.py:316
  50.1 23.9 %collective-permute-start.6 = (bf16[576,256]{1,0:T(8,128)(2,1)S(1)}, bf16[576,256]{1,0:T(8,128)(2,1)S(1)}, u32[]{:S(2)}, u32[]{:S(2)}) collective-permute-start(bf16[576,256]{1,0:T(8,128)(2,1)S(1)} %copy-done.11), channel_id=1, source_target_pairs={{0,2},{1,3},{2,0},{3,1},{4,6},{5,7},{6,4},{7,5},{8,10},{9,11},{10,... | collective-permute-start | bytes 884744 | tf_op jit(solution)/shard_map/ppermute | solution.py:316
  51.3 22.7 %collective-permute-start.5 = (bf16[576,256]{1,0:T(8,128)(2,1)S(1)}, bf16[576,256]{1,0:T(8,128)(2,1)S(1)}, u32[]{:S(2)}, u32[]{:S(2)}) collective-permute-start(bf16[576,256]{1,0:T(8,128)(2,1)S(1)} %copy-done.10), channel_id=1, source_target_pairs={{0,4},{1,5},{2,6},{3,7},{4,0},{5,1},{6,2},{7,3},{8,12},{9,13},{10,... | collective-permute-start | bytes 884744 | tf_op jit(solution)/shard_map/ppermute | solution.py:316
  74.0 33.3 %collective-permute-start.11 = (bf16[576,256]{1,0:T(8,128)(2,1)S(1)}, bf16[576,256]{1,0:T(8,128)(2,1)S(1)}, u32[]{:S(2)}, u32[]{:S(2)}) collective-permute-start(bf16[576,256]{1,0:T(8,128)(2,1)S(1)} %copy-done.9), channel_id=1, source_target_pairs={{0,5},{1,4},{2,7},{3,6},{4,1},{5,0},{6,3},{7,2},{8,13},{9,12},{10,... | collective-permute-start | bytes 884744 | tf_op jit(solution)/shard_map/ppermute | solution.py:316
  74.8 32.5 %collective-permute-start.12 = (bf16[576,256]{1,0:T(8,128)(2,1)S(1)}, bf16[576,256]{1,0:T(8,128)(2,1)S(1)}, u32[]{:S(2)}, u32[]{:S(2)}) collective-permute-start(bf16[576,256]{1,0:T(8,128)(2,1)S(1)} %copy-done.8), channel_id=1, source_target_pairs={{0,6},{1,7},{2,4},{3,5},{4,2},{5,3},{6,0},{7,1},{8,14},{9,15},{10,... | collective-permute-start | bytes 884744 | tf_op jit(solution)/shard_map/ppermute | solution.py:316
  76.0 22.3 %collective-permute-start.8 = (bf16[448,256]{1,0:T(8,128)(2,1)S(1)}, bf16[448,256]{1,0:T(8,128)(2,1)S(1)}, u32[]{:S(2)}, u32[]{:S(2)}) collective-permute-start(bf16[448,256]{1,0:T(8,128)(2,1)S(1)} %copy-done.16), channel_id=1, source_target_pairs={{0,12},{1,13},{2,14},{3,15},{4,8},{5,9},{6,10},{7,11},{8,4},{9,5},... | collective-permute-start | bytes 688136 | tf_op jit(solution)/shard_map/ppermute | solution.py:316
  80.6 20.8 %collective-permute-start.9 = (bf16[448,256]{1,0:T(8,128)(2,1)S(1)}, bf16[448,256]{1,0:T(8,128)(2,1)S(1)}, u32[]{:S(2)}, u32[]{:S(2)}) collective-permute-start(bf16[448,256]{1,0:T(8,128)(2,1)S(1)} %copy-done.15), channel_id=1, source_target_pairs={{0,13},{1,12},{2,15},{3,14},{4,9},{5,8},{6,11},{7,10},{8,5},{9,4},... | collective-permute-start | bytes 688136 | tf_op jit(solution)/shard_map/ppermute | solution.py:316
  80.7 26.6 %collective-permute-start.10 = (bf16[448,256]{1,0:T(8,128)(2,1)S(1)}, bf16[448,256]{1,0:T(8,128)(2,1)S(1)}, u32[]{:S(2)}, u32[]{:S(2)}) collective-permute-start(bf16[448,256]{1,0:T(8,128)(2,1)S(1)} %copy-done.14), channel_id=1, source_target_pairs={{0,14},{1,15},{2,12},{3,13},{4,10},{5,11},{6,8},{7,9},{8,6},{9,7},... | collective-permute-start | bytes 688136 | tf_op jit(solution)/shard_map/ppermute | solution.py:316
  107.3 20.9 %collective-permute-start.14 = (bf16[576,256]{1,0:T(8,128)(2,1)S(1)}, bf16[576,256]{1,0:T(8,128)(2,1)S(1)}, u32[]{:S(2)}, u32[]{:S(2)}) collective-permute-start(bf16[576,256]{1,0:T(8,128)(2,1)S(1)} %copy-done.7), channel_id=1, source_target_pairs={{0,7},{1,6},{2,5},{3,4},{4,3},{5,2},{6,1},{7,0},{8,15},{9,14},{10,... | collective-permute-start | bytes 884744 | tf_op jit(solution)/shard_map/ppermute | solution.py:316
  110.8 17.5 %collective-permute-start.15 = (bf16[576,256]{1,0:T(8,128)(2,1)S(1)}, bf16[576,256]{1,0:T(8,128)(2,1)S(1)}, u32[]{:S(2)}, u32[]{:S(2)}) collective-permute-start(bf16[576,256]{1,0:T(8,128)(2,1)S(1)} %copy-done.6), channel_id=1, source_target_pairs={{0,1},{1,0},{2,3},{3,2},{4,5},{5,4},{6,7},{7,6},{8,9},{9,8},{10,11... | collective-permute-start | bytes 884744 | tf_op jit(solution)/shard_map/ppermute | solution.py:316
  111.8 16.4 %collective-permute-start.13 = (bf16[448,256]{1,0:T(8,128)(2,1)S(1)}, bf16[448,256]{1,0:T(8,128)(2,1)S(1)}, u32[]{:S(2)}, u32[]{:S(2)}) collective-permute-start(bf16[448,256]{1,0:T(8,128)(2,1)S(1)} %copy-done.13), channel_id=1, source_target_pairs={{0,15},{1,14},{2,13},{3,12},{4,11},{5,10},{6,9},{7,8},{8,7},{9,6},... | collective-permute-start | bytes 688136 | tf_op jit(solution)/shard_map/ppermute | solution.py:316
